TPU v7x, 32 devices: a whole 2x2x4 slice. The times are simulated.
32 devices in a mesh: parts: 2 (over x), dp: 8 (over z, y), layer: 2 (over core).
Axes of the slice: x: 2, y: 2, z: 4, core: 2. Of those that a mesh axis runs over, the one named last changes fastest.
Arguments:
- train_acts: bfloat16 [16, 4, 256, 4096], P(('parts', 'dp'), 'layer'), parts along dimension 0, may hold values from -6 to 6
- train_grads: bfloat16 [16, 4, 256, 4096], P(('parts', 'dp'), 'layer'), parts along dimension 0
- train_lengths: int32 [16], P(('parts', 'dp')), parts along dimension 0, may hold values from 32 to 256, as said below
- query_log: bfloat16 [256, 4, 4096], P('dp', 'layer'), may hold values from -4 to 4
- proj_in: bfloat16 [4, 64, 4096], P('layer')
- proj_out: bfloat16 [4, 64, 4096], P('layer')
- basis_in: float32 [32, 64, 64], replicated, as said below
- basis_out: float32 [32, 64, 64], replicated, as said below
- layer_ids: int32 [4], P('layer'), may hold values from 0 to 31, as said below
Outputs:
- scores: float32 [16, 256], P(('parts', 'dp'), 'layer'), parts along dimension 0
There are 2 independent parts, one for each index of `parts`. A program takes and returns all parts, laid end to end along the dimension named above; an argument that names none is the same for every part. Nothing has to cross between parts.
Inputs may be any that keep to these rules, and one draw needn't show every extreme that they name: `train_lengths`: at least one train sequence has exactly 256 live tokens and another exactly one eighth of 256. `layer_ids`: distinct layer numbers below 32; one of them is 31. `basis_in`: each [64, 64] matrix is orthogonal. `basis_out`: each [64, 64] matrix is orthogonal.
All inputs are finite; a program needn't handle non-finite values.
Results may differ from a plain program's by a relative error of at most 0.0041.
Values may be sent and summed in bfloat16 or wider, within the bound.
A program may use at most 128 MiB of HBM per device.

v0:
```python
import jax
import jax.numpy as jnp
from jax import lax
from jax.sharding import PartitionSpec as P


def rotate(frames_out, frames_in, matrices):
    highest = lax.Precision.HIGHEST
    left_turn = jnp.einsum("lca,slcd->slad", frames_out, matrices, precision=highest)
    return jnp.einsum("slad,ldb->slab", left_turn, frames_in, precision=highest)


def per_device(
    train_acts,
    train_grads,
    train_lengths,
    query_log,
    proj_in,
    proj_out,
    basis_in,
    basis_out,
    layer_ids,
):
    highest = lax.Precision.HIGHEST
    seq_count, layer_count, seq_length, model_width = train_acts.shape
    proj_rank = proj_in.shape[1]
    query_count = query_log.shape[0]
    table_layers = basis_in.shape[0]
    dp_size = lax.axis_size("dp")
    selector = (
        layer_ids[:, None] == lax.broadcasted_iota(jnp.int32, (layer_count, table_layers), 1)
    ).astype(jnp.float32)
    frames_in = jnp.einsum("ln,nab->lab", selector, basis_in, precision=highest)
    frames_out = jnp.einsum("ln,nab->lab", selector, basis_out, precision=highest)
    query_mat = query_log.astype(jnp.float32).reshape(
        query_count, layer_count, proj_rank, proj_rank
    )
    query_turn = rotate(frames_out, frames_in, query_mat)
    token_mask = (
        lax.broadcasted_iota(jnp.int32, (seq_count, seq_length), 1) < train_lengths[:, None]
    ).astype(jnp.float32)
    low_in = jnp.einsum("lrd,sltd->slrt", proj_in, train_acts, preferred_element_type=jnp.float32)
    low_out = jnp.einsum(
        "lrd,sltd->slrt", proj_out, train_grads, preferred_element_type=jnp.float32
    )
    low_out = low_out * token_mask[:, None, None, :]
    outer = jnp.einsum("slat,slbt->slab", low_out, low_in, precision=highest)
    turned = rotate(frames_out, frames_in, outer)
    energy_part = jnp.sum(turned * turned, axis=0)
    energy = lax.psum(energy_part, "dp") / (seq_count * dp_size)
    damping = 0.1 * jnp.mean(energy, axis=(1, 2)) + 1e-06
    divisor = (energy + damping[:, None, None])[None]
    train_rot = turned.astype(jnp.bfloat16).reshape(seq_count, layer_count, proj_rank * proj_rank)
    query_damped = (
        (query_turn / divisor)
        .astype(jnp.bfloat16)
        .reshape(query_count, layer_count, proj_rank * proj_rank)
    )
    partial_value = jnp.einsum(
        "slk,plk->sp",
        train_rot,
        lax.all_gather(query_damped, "dp", axis=0, tiled=True),
        preferred_element_type=jnp.float32,
    )
    summed = lax.psum(partial_value, "layer")
    share_cols = summed.shape[1] // lax.axis_size("layer")
    first_col = lax.axis_index("layer") * share_cols
    return lax.dynamic_slice_in_dim(summed, first_col, share_cols, 1)


def solution(mesh):
    return jax.shard_map(
        per_device,
        mesh=mesh,
        in_specs=(
            P(("parts", "dp"), "layer", None, None),
            P(("parts", "dp"), "layer", None, None),
            P(("parts", "dp")),
            P("dp", "layer", None),
            P("layer", None, None),
            P("layer", None, None),
            P(),
            P(),
            P("layer"),
        ),
        out_specs=P(("parts", "dp"), "layer"),
        check_vma=False,
    )
```

profile of v0, /device:TPU:0, one launch (start us, length us, event | category | flops | bytes accessed | tf_op | source)
XLA Modules:
  0.0 153.1 jit_solution(5366761829016885089)
XLA Ops:
  6.5 0.0 copy-start
  6.5 0.0 all-gather.2.cloned.1.call-start
  7.3 2.2 %fusion.23 = f32[2,64,64]{2,0,1:T(2,128)S(1)} fusion(f32[32,64,64]{2,1,0:T(8,128)} %param.16, s32[2]{0:T(128)} %param.17), kind=kOutput, calls=%fused_computation.16 | convolution fusion | flops 3145792 | bytes 557064 | tf_op jit(solution)/shard_map/ln,nab->lab/dot_general | solution.py:34
  9.5 0.0 copy-start.2
  9.5 2.3 %fusion.25 = f32[2,64,64]{2,0,1:T(2,128)S(1)} fusion(f32[32,64,64]{2,1,0:T(8,128)} %param.15, s32[2]{0:T(128)} %param.17), kind=kOutput, calls=%fused_computation.18 | convolution fusion | flops 3145792 | bytes 557064 | tf_op jit(solution)/shard_map/ln,nab->lab/dot_general | solution.py:33
  11.9 2.3 %reshape.62 = bf16[32,2,64,64]{3,2,1,0:T(8,128)(2,1)S(1)} reshape(bf16[32,2,4096]{2,1,0:T(2,128)(2,1)} %param.12) | data formatting | bytes 1048576 | tf_op jit(solution)/shard_map/reshape | solution.py:35
  14.2 0.0 copy-done
  14.2 0.0 copy-start.1
  14.2 3.7 %fusion.12 = f32[2,64,256]{2,1,0:T(8,128)S(1)} fusion(bf16[2,64,4096]{2,1,0:T(8,128)(2,1)S(1)} %copy-done, bf16[1,2,256,4096]{3,2,1,0:T(8,128)(2,1)} %param.9), kind=kOutput, calls=%fused_computation.9 | convolution fusion | flops 268435456 | bytes 5373952 | tf_op jit(solution)/shard_map/lrd,sltd->slrt/dot_general | solution.py:42
  17.9 0.0 copy-done.2
  17.9 0.0 copy-done.1
  17.9 1.4 fusion.18
  19.3 0.3 fusion.38
  19.6 0.2 convolution_bitcast_fusion
  19.8 0.3 multiply_bitcast_fusion
  20.1 39.3 %psum.14 = f32[2,64,64]{1,2,0:T(8,128)S(1)} all-reduce(f32[2,64,64]{1,2,0:T(8,128)S(1)} %get-tuple-element.5), channel_id=1, replica_groups=mesh['parts'=2,'dp'=8,'layer'=2] {'dp'}, use_global_device_ids=true, to_apply=%region_0.0 | all-reduce | flops 8192 | bytes 65536 | tf_op jit(solution)/shard_map/psum | solution.py:50
  59.4 0.1 multiply_reduce_fusion
  59.5 0.1 multiply_add_fusion
  59.6 1.1 fusion.21
  60.7 6.1 %fusion.4 = bf16[32,2,64,64]{2,3,0,1:T(8,128)(2,1)S(1)} fusion(f32[2,64,32,64]{3,1,2,0:T(8,128)S(1)} %fusion.21, f32[2,64,64]{1,2,0:T(8,128)S(1)} %multiply_add_fusion, f32[2,64,64,1]{2,0,1,3:T(2,128)S(1)} %bitcast.83), kind=kOutput, calls=%fused_computation.5 | convolution fusion | flops 201850880 | bytes 1638400 | tf_op jit(solution)/shard_map/slad,ldb->slab/dot_general | solution.py:10
  66.8 0.7 copy.23
  67.5 1.6 %reshape.63 = bf16[32,2,4096]{2,0,1:T(8,128)(2,1)} reshape(bf16[32,2,64,64]{3,2,0,1:T(8,128)(2,1)S(1)} %copy.23) | data formatting | bytes 1048576 | tf_op jit(solution)/shard_map/reshape | solution.py:57
  69.1 0.0 all-gather.2.cloned.1.call-update
  69.1 0.1 copy.21
  69.2 0.1 reshape.70
  69.3 70.6 %all-gather.2.cloned.1.call-done = bf16[256,2,4096]{2,0,1:T(8,128)(2,1)} async-done(((bf16[32,2,4096]{2,0,1:T(8,128)(2,1)}), bf16[256,2,4096]{2,0,1:T(8,128)(2,1)}) %all-gather.2.cloned.1.call-update) | async-done | bytes 4194320 | tf_op jit(solution)/shard_map/all_gather | solution.py:62
  139.9 3.4 %convolution_bitcast_fusion.1 = f32[1,256]{1,0:T(1,128)S(1)} fusion(bf16[2,4096,1]{1,2,0:T(2,128)(2,1)S(1)} %reshape.70, bf16[256,2,4096]{2,0,1:T(8,128)(2,1)} %all-gather.2.cloned.1.call-done), kind=kOutput, calls=%fused_computation.13 | convolution fusion | flops 4194304 | bytes 4211712 | tf_op jit(solution)/shard_map/slk,plk->sp/dot_general | solution.py:59
  143.3 2.5 %psum.15 = f32[1,256]{1,0:T(1,128)S(1)} all-reduce(f32[1,256]{1,0:T(1,128)S(1)} %convolution_bitcast_fusion.1), channel_id=1, replica_groups=mesh['parts'=2,'dp'=8,'layer'=2] {'layer'}, use_global_device_ids=true, to_apply=%region_2.0 | all-reduce | flops 256 | bytes 2048 | tf_op jit(solution)/shard_map/psum | solution.py:65
  145.8 0.5 constant_dynamic-slice_fusion
  (2 shorter events, 0.0 us)
Async XLA Ops:
  6.5 7.6 %copy-start = (bf16[2,64,4096]{2,1,0:T(8,128)(2,1)S(1)}, bf16[2,64,4096]{2,1,0:T(8,128)(2,1)}, u32[]{:S(2)}) copy-start(bf16[2,64,4096]{2,1,0:T(8,128)(2,1)} %param.13) | copy-start | bytes 3145732
  6.5 133.4 %all-gather.2.cloned.1.call-start = ((), (), s32[]{:S(2)}) async-start(), calls=%async_computation | async-start | bytes 4718592 | tf_op jit(solution)/shard_map/all_gather | solution.py:62
  9.5 8.4 %copy-start.2 = (bf16[2,64,4096]{2,1,0:T(8,128)(2,1)S(1)}, bf16[2,64,4096]{2,1,0:T(8,128)(2,1)}, u32[]{:S(2)}) copy-start(bf16[2,64,4096]{2,1,0:T(8,128)(2,1)} %param.14) | copy-start | bytes 3145732
  14.2 3.8 %copy-start.1 = (bf16[1,2,256,4096]{3,2,1,0:T(8,128)(2,1)S(1)}, bf16[1,2,256,4096]{3,2,1,0:T(8,128)(2,1)}, u32[]{:S(2)}) copy-start(bf16[1,2,256,4096]{3,2,1,0:T(8,128)(2,1)} %param.10) | copy-start | bytes 12582916
Sparse Core Ops, SparseCore 0:
  69.2 70.6 all-gather.1
where the time goes:
time: 153 us
  waiting for transfers between devices  70.6 us (46%)
  blocking collectives  41.8 us (27%)
  matrix products  21 us (14%)
  between operations  14.3 us (9%)
  local copies, waits for them, and re-layouts  5.28 us (3%)
    all_gather x1, waiting for transfers between devices, per_device(): lax.all_gather(query_damped, 'dp', axis=0, tiled=True)  70.6 us
    psum x1, blocking collectives, per_device(): energy = lax.psum(energy_part, 'dp') / (seq_count * dp_size)  39.3 us
    dot_general x2, matrix products, rotate(): return jnp.einsum('slad,ldb->slab', left_turn, frames_in, precision=highest)  6.44 us
    dot_general x1, matrix products, per_device(): jnp.einsum('lrd,sltd->slrt', proj_in, train_acts, preferred_element_type=...  3.73 us
    dot_general x1, matrix products, per_device(): jnp.einsum('slk,plk->sp', train_rot, lax.all_gather(query_damped, 'dp', a...  3.39 us
  transfers between devices with their start and end apart: 1, of which 1 were waited for; matrix products, arithmetic and copies ran while one was open for 0% of the time, Pallas kernels for 0%

commit v1 on v0

v1 whole, which is shorter than its diff:
```python
import functools

import jax
import jax.numpy as jnp
from jax import lax
from jax.experimental import pallas as pl
from jax.experimental.pallas import tpu as pltpu
from jax.sharding import PartitionSpec as P

F32 = jnp.float32
BF16 = jnp.bfloat16
MESH = pl.DeviceIdType.MESH
NN = (((1,), (0,)), ((), ()))
NT = (((1,), (1,)), ((), ()))


def dot(a, b, dims=NN):
    return lax.dot_general(a, b, dims, preferred_element_type=F32)


def split(a):
    hi = a.astype(BF16)
    return hi, (a - hi.astype(F32)).astype(BF16)


def dot3(a, b, dims=NN):
    ah, al = split(a)
    bh, bl = split(b)
    return dot(ah, bh, dims) + (dot(ah, bl, dims) + dot(al, bh, dims))


def kernel(
    n, layers, lens, lids, acts, grads, query, pin, pout, bin_, bout, out,
    abuf, gbuf, pibuf, pobuf, qbuf, bibuf, bobuf, tbuf, wbuf, sbuf, rbuf,
    load_sem, send_sem, recv_sem, send2_sem, recv2_sem,
):
    part = lax.axis_index("parts")
    me = lax.axis_index("dp")
    core = lax.axis_index("layer")
    half = n // layers
    mine = me // half
    rank = pibuf.shape[1]
    qpd = qbuf.shape[1]
    tokens = abuf.shape[1]

    barrier = pltpu.get_barrier_semaphore()
    for off in range(n):
        for lay in range(layers):
            if off == 0 and lay == 0:
                continue
            pl.semaphore_signal(
                barrier, inc=1,
                device_id=(part, lax.rem(me + off, n), lax.rem(core + lay, layers)),
                device_id_type=MESH,
            )

    loads = []

    def load(src, dst):
        c = pltpu.make_async_copy(src, dst, load_sem.at[len(loads)])
        c.start()
        loads.append(c)
        return c

    lp = []
    for l in range(2):
        a = load(pout.at[l], pobuf.at[l])
        b = load(grads.at[0, l], gbuf.at[l])
        c = load(pin.at[l], pibuf.at[l])
        d = load(acts.at[0, l], abuf.at[l])
        if l == 0:
            e = (load(bin_, bibuf), load(bout, bobuf))
        lp.append((a, b, c, d))
    lq = load(query, qbuf)

    length = lens[0]
    live = lax.broadcasted_iota(jnp.int32, (rank, tokens), 1) < length
    frames_in, frames_out, turned = [], [], []
    for l in range(2):
        a, b, c, d = lp[l]
        a.wait()
        b.wait()
        low_out = dot(pobuf[l], gbuf[l], NT)
        low_out = jnp.where(live, low_out, 0.0)
        c.wait()
        d.wait()
        low_in = dot(abuf[l], pibuf[l], NT)
        if l == 0:
            e[0].wait()
            e[1].wait()
        v = bibuf[lids[l]]
        u = bobuf[lids[l]]
        frames_in.append(v)
        frames_out.append(u)
        outer = dot3(low_out, low_in)
        turned.append(dot3(dot3(u.T, outer), v))
    tbuf[me] = jnp.concatenate(turned, axis=1).astype(BF16)

    peers = (n * layers) - 1
    pl.semaphore_wait(barrier, peers)

    def gather(off):
        to = lax.rem(me + off, n)
        return pltpu.make_async_remote_copy(
            src_ref=tbuf.at[me], dst_ref=tbuf.at[me],
            send_sem=send_sem.at[off - 1], recv_sem=recv_sem.at[off - 1],
            device_id=(part, to, core), device_id_type=MESH,
        )

    def arrived(off):
        frm = lax.rem(me + n - off, n)
        return pltpu.make_async_remote_copy(
            src_ref=tbuf.at[frm], dst_ref=tbuf.at[frm],
            send_sem=send_sem.at[off - 1], recv_sem=recv_sem.at[off - 1],
            device_id=(part, frm, core), device_id_type=MESH,
        )

    for off in range(1, n):
        gather(off).start()

    zero = jnp.zeros((rank, rank), F32)
    v0 = jnp.concatenate([frames_in[0], zero], axis=1)
    v1 = jnp.concatenate([zero, frames_in[1]], axis=1)
    right = jnp.concatenate([v0, v0, v1, v1], axis=0)
    lq.wait()

    for off in range(1, n):
        arrived(off).wait_recv()

    t = tbuf[...].astype(F32)
    energy = jnp.sum(t * t, axis=0) * (1.0 / n)
    first = lax.broadcasted_iota(jnp.int32, energy.shape, 1) < rank
    sum0 = jnp.sum(jnp.where(first, energy, 0.0))
    sum1 = jnp.sum(jnp.where(first, 0.0, energy))
    damping = jnp.where(first, sum0, sum1) * (0.1 / (rank * rank)) + 1e-6
    scaled = t * (1.0 / (energy + damping))[None]
    y = dot3(scaled.reshape(n * rank, 2 * rank), right, NT)
    wide = 2 * rank
    lanes = lax.broadcasted_iota(jnp.int32, (n, wide), 1) < rank
    total = None
    for l in range(2):
        yl = jnp.concatenate(
            [y[s * rank:(s + 1) * rank, l * wide:(l + 1) * wide] for s in range(n)], axis=1
        )
        w = dot3(frames_out[l], yl)
        for s in range(n):
            wbuf[l, s * rank:(s + 1) * rank, :] = w[:, s * wide:(s + 1) * wide]
        tiles = []
        for j in range(rank // 2):
            even = wbuf[l, pl.ds(2 * j, n, stride=rank), :]
            odd = wbuf[l, pl.ds(2 * j + 1, n, stride=rank), :]
            tiles.append(jnp.where(lanes, even, odd))
        flat = jnp.concatenate(tiles, axis=1)
        hi = flat.astype(BF16).astype(F32)
        both = jnp.concatenate([hi, flat - hi], axis=0).astype(BF16)
        p = dot(both, qbuf[l], NT)
        p = p[:n] + p[n:]
        total = p if total is None else total + p
    if qpd < 128:
        total = jnp.concatenate([total, jnp.zeros((n, 128 - qpd), F32)], axis=1)
    for s in range(n):
        sbuf[s] = total[s:s + 1]

    slot = core * half + lax.rem(me, half)

    def deliver(off):
        to = lax.rem(me + off, n)
        return pltpu.make_async_remote_copy(
            src_ref=sbuf.at[to], dst_ref=rbuf.at[slot],
            send_sem=send2_sem.at[off], recv_sem=recv2_sem.at[slot],
            device_id=(part, to, mine), device_id_type=MESH,
        )

    for off in range(1, n):
        deliver(off).start()

    @pl.when(mine == core)
    def _():
        rbuf[slot] = sbuf[me]

    @pl.when(mine != core)
    def _():
        deliver(0).start()

    for lay in range(layers):
        for j in range(half):
            src = core * half + j
            own = jnp.logical_and(src == me, core == lay)

            @pl.when(jnp.logical_not(own))
            def _(lay=lay, j=j):
                k = lay * half + j
                pltpu.make_async_remote_copy(
                    src_ref=sbuf.at[0], dst_ref=rbuf.at[k],
                    send_sem=send2_sem.at[0], recv_sem=recv2_sem.at[k],
                    device_id=(part, me, mine), device_id_type=MESH,
                ).wait_recv()

    pieces = []
    for j in range(half):
        acc = rbuf[j]
        for lay in range(1, layers):
            acc = acc + rbuf[lay * half + j]
        pieces.append(acc[:, :qpd])
    out[...] = jnp.concatenate(pieces, axis=1)

    for off in range(1, n):
        gather(off).wait_send()
        deliver(off).wait_send()

    @pl.when(mine != core)
    def _():
        deliver(0).wait_send()


def per_device(acts, grads, lens, query, pin, pout, bin_, bout, lids):
    n = lax.axis_size("dp")
    layers = lax.axis_size("layer")
    _, held, tokens, width = acts.shape
    rank = pin.shape[1]
    qpd = query.shape[0]
    query = jnp.swapaxes(query, 0, 1)
    hbm = pl.BlockSpec(memory_space=pl.ANY)
    smem = pl.BlockSpec(memory_space=pltpu.SMEM)
    return pl.pallas_call(
        functools.partial(kernel, n, layers),
        out_shape=jax.ShapeDtypeStruct((1, n * qpd // layers), F32),
        in_specs=[smem, smem] + [hbm] * 7,
        out_specs=pl.BlockSpec(memory_space=pltpu.VMEM),
        scratch_shapes=[
            pltpu.VMEM((held, tokens, width), BF16),
            pltpu.VMEM((held, tokens, width), BF16),
            pltpu.VMEM(pin.shape, BF16),
            pltpu.VMEM(pin.shape, BF16),
            pltpu.VMEM(query.shape, BF16),
            pltpu.VMEM(bin_.shape, F32),
            pltpu.VMEM(bout.shape, F32),
            pltpu.VMEM((n, rank, held * rank), BF16),
            pltpu.VMEM((held, n * rank, 2 * rank), F32),
            pltpu.VMEM((n, 1, 128), F32),
            pltpu.VMEM((n, 1, 128), F32),
            pltpu.SemaphoreType.DMA((11,)),
            pltpu.SemaphoreType.DMA((n - 1,)),
            pltpu.SemaphoreType.DMA((n - 1,)),
            pltpu.SemaphoreType.DMA((n,)),
            pltpu.SemaphoreType.DMA((n,)),
        ],
        compiler_params=pltpu.CompilerParams(
            collective_id=0, has_side_effects=True, vmem_limit_bytes=48 * 2**20
        ),
    )(lens, lids, acts, grads, query, pin, pout, bin_, bout)


def solution(mesh):
    return jax.shard_map(
        per_device,
        mesh=mesh,
        in_specs=(
            P(("parts", "dp"), "layer", None, None),
            P(("parts", "dp"), "layer", None, None),
            P(("parts", "dp")),
            P("dp", "layer", None),
            P("layer", None, None),
            P("layer", None, None),
            P(),
            P(),
            P("layer"),
        ),
        out_specs=P(("parts", "dp"), "layer"),
        check_vma=False,
    )
```

time: 153 us -> 29.4 us (0.19)
  waiting for transfers between devices: 70.6 us -> 0 us
  blocking collectives: 41.8 us -> 0 us
  matrix products: 21 us -> 0 us
  Pallas kernels: 0 us -> 21 us
  between operations: 14.3 us -> 0.68 us
  local copies, waits for them, and re-layouts: 5.28 us -> 7.4 us
    all_gather x1 -> x0, waiting for transfers between devices: 70.6 us -> none  [per_device(): lax.all_gather(query_damped, 'dp', axis=0, tiled=True)]
    psum x2 -> x0, blocking collectives: 41.8 us -> none  [the longest x1 39.3 us: per_device(): energy = lax.psum(energy_part, 'dp') / (seq_count * dp_size)]
    dot_general x10 -> x0, matrix products: 21 us -> none  [the longest x2 6.44 us: rotate(): return jnp.einsum('slad,ldb->slab', left_turn, frames_in, precision=highest)]
    pallas_call x0 -> x1, Pallas kernels: none -> 21 us  [per_device(): pl.pallas_call(functools.partial(kernel, n, layers), out_shape=jax.ShapeD...]
    unnamed x6 -> x12, local copies, waits for them, and re-layouts: 0.02 us -> 7.4 us
    reshape x2 -> x0, local copies, waits for them, and re-layouts: 3.91 us -> none  [the longest x1 2.3 us: per_device(): query_log.astype(jnp.float32)]
  transfers between devices with their start and end apart: 1 -> 0, of which waited for: 1 -> 0; matrix products, arithmetic and copies ran while one was open for 0% -> 0% of each run, Pallas kernels for 0% -> 0%
where the time goes in v1:
time: 29.4 us; the launch traced here: 29.1 us
  Pallas kernels  21 us (71%)
  local copies, waits for them, and re-layouts  7.4 us (25%)
  between operations  0.68 us (2%)
    pallas_call x1, Pallas kernels, per_device(): pl.pallas_call(functools.partial(kernel, n, layers), out_shape=jax.ShapeD...  21 us
    unnamed x12, local copies, waits for them, and re-layouts  7.4 us

profile of v1, /device:TPU:0, one launch (start us, length us, event | category | flops | bytes accessed | tf_op | source)
XLA Modules:
  0.0 29.1 jit_solution(5159213217205523903)
XLA Ops:
  0.7 1.3 %copy.12 = bf16[32,2,4096]{2,0,1:T(8,128)(2,1)S(1)} copy(bf16[32,2,4096]{2,1,0:T(2,128)(2,1)} %param.12) | data formatting | bytes 1048576 | tf_op args[3]
  2.0 0.0 copy-start
  2.0 1.2 %copy-done = bf16[2,64,4096]{2,1,0:T(8,128)(2,1)S(1)} copy-done((bf16[2,64,4096]{2,1,0:T(8,128)(2,1)S(1)}, bf16[2,64,4096]{2,1,0:T(8,128)(2,1)}, u32[]{:S(2)}) %copy-start) | copy-done | bytes 1048600
  3.2 0.0 copy-start.1
  3.2 1.2 %copy-done.1 = bf16[2,64,4096]{2,1,0:T(8,128)(2,1)S(1)} copy-done((bf16[2,64,4096]{2,1,0:T(8,128)(2,1)S(1)}, bf16[2,64,4096]{2,1,0:T(8,128)(2,1)}, u32[]{:S(2)}) %copy-start.1) | copy-done | bytes 1048600
  4.4 0.0 copy-start.2
  4.4 1.2 %copy-done.2 = f32[32,64,64]{2,1,0:T(8,128)S(1)} copy-done((f32[32,64,64]{2,1,0:T(8,128)S(1)}, f32[32,64,64]{2,1,0:T(8,128)}, u32[]{:S(2)}) %copy-start.2) | copy-done | bytes 524312
  5.7 0.0 copy-start.3
  5.7 1.2 %copy-done.3 = f32[32,64,64]{2,1,0:T(8,128)S(1)} copy-done((f32[32,64,64]{2,1,0:T(8,128)S(1)}, f32[32,64,64]{2,1,0:T(8,128)}, u32[]{:S(2)}) %copy-start.3) | copy-done | bytes 524312
  6.9 0.0 copy-start.4
  6.9 0.7 %copy-done.4 = s32[2]{0:T(128)S(1)} copy-done((s32[2]{0:T(128)S(1)}, s32[2]{0:T(128)}, u32[]{:S(2)}) %copy-start.4) | copy-done | bytes 32
  7.5 21.0 %shard_map.91 = f32[1,128]{1,0:T(1,128)S(1)} custom-call(s32[1]{0:T(128)S(6)} %copy.14.lens, s32[2]{0:T(128)S(1)} %copy-done.4, bf16[1,2,256,4096]{3,2,1,0:T(8,128)(2,1)} %acts.1, bf16[1,2,256,4096]{3,2,1,0:T(8,128)(2,1)} %grads.1, bf16[2,32,4096]{2,1,0:T(8,128)(2,1)S(1)} %bitcast.3, bf16[2,64,4096]{2,1,0:T(8,128)(2,1)S(1)} %copy-done, ...), custom_call_target="tpu_custom_call" | custom-call | tf_op jit(solution)/shard_map/pallas_call | solution.py:225
  28.5 0.5 %copy.15 = f32[1,128]{1,0:T(1,128)} copy(f32[1,128]{1,0:T(1,128)S(1)} %shard_map.91) | data formatting | bytes 1024
Async XLA Ops:
  2.0 1.2 %copy-start = (bf16[2,64,4096]{2,1,0:T(8,128)(2,1)S(1)}, bf16[2,64,4096]{2,1,0:T(8,128)(2,1)}, u32[]{:S(2)}) copy-start(bf16[2,64,4096]{2,1,0:T(8,128)(2,1)} %pin.1) | copy-start | bytes 3145732
  3.2 1.2 %copy-start.1 = (bf16[2,64,4096]{2,1,0:T(8,128)(2,1)S(1)}, bf16[2,64,4096]{2,1,0:T(8,128)(2,1)}, u32[]{:S(2)}) copy-start(bf16[2,64,4096]{2,1,0:T(8,128)(2,1)} %pout.1) | copy-start | bytes 3145732
  4.4 1.2 %copy-start.2 = (f32[32,64,64]{2,1,0:T(8,128)S(1)}, f32[32,64,64]{2,1,0:T(8,128)}, u32[]{:S(2)}) copy-start(f32[32,64,64]{2,1,0:T(8,128)} %bin_.1) | copy-start | bytes 1572868
  5.7 1.2 %copy-start.3 = (f32[32,64,64]{2,1,0:T(8,128)S(1)}, f32[32,64,64]{2,1,0:T(8,128)}, u32[]{:S(2)}) copy-start(f32[32,64,64]{2,1,0:T(8,128)} %bout.1) | copy-start | bytes 1572868
  6.9 0.7 %copy-start.4 = (s32[2]{0:T(128)S(1)}, s32[2]{0:T(128)}, u32[]{:S(2)}) copy-start(s32[2]{0:T(128)} %lids.1) | copy-start | bytes 28

commit v2 on v1

--- a/solution.py
+++ b/solution.py
@@ -31,7 +31,7 @@
 
 def kernel(
     n, layers, lens, lids, acts, grads, query, pin, pout, bin_, bout, out,
-    abuf, gbuf, pibuf, pobuf, qbuf, bibuf, bobuf, tbuf, wbuf, sbuf, rbuf,
+    abuf, gbuf, pibuf, pobuf, xbuf, fbuf, qbuf, bibuf, bobuf, tbuf, wbuf, sbuf, rbuf,
     load_sem, send_sem, recv_sem, send2_sem, recv2_sem,
 ):
     part = lax.axis_index("parts")
@@ -40,7 +40,7 @@
     half = n // layers
     mine = me // half
     rank = pibuf.shape[1]
-    qpd = qbuf.shape[1]
+    qpd = query.shape[0]
     tokens = abuf.shape[1]
 
     barrier = pltpu.get_barrier_semaphore()
@@ -71,7 +71,7 @@
         if l == 0:
             e = (load(bin_, bibuf), load(bout, bobuf))
         lp.append((a, b, c, d))
-    lq = load(query, qbuf)
+    lq = load(query, xbuf)
 
     length = lens[0]
     live = lax.broadcasted_iota(jnp.int32, (rank, tokens), 1) < length
@@ -123,6 +123,14 @@
     v1 = jnp.concatenate([zero, frames_in[1]], axis=1)
     right = jnp.concatenate([v0, v0, v1, v1], axis=0)
     lq.wait()
+    rows = xbuf[...].reshape(2 * qpd, xbuf.shape[2])
+    for j in range(fbuf.shape[0]):
+        fbuf[j] = rows[:, j * 128:(j + 1) * 128].astype(F32)
+    for l in range(2):
+        for j in range(fbuf.shape[0]):
+            qbuf[l, :, j * 128:(j + 1) * 128] = fbuf[
+                j, pl.ds(l, qpd, stride=2), :
+            ].astype(BF16)
 
     for off in range(1, n):
         arrived(off).wait_recv()
@@ -219,7 +227,6 @@
     _, held, tokens, width = acts.shape
     rank = pin.shape[1]
     qpd = query.shape[0]
-    query = jnp.swapaxes(query, 0, 1)
     hbm = pl.BlockSpec(memory_space=pl.ANY)
     smem = pl.BlockSpec(memory_space=pltpu.SMEM)
     return pl.pallas_call(
@@ -233,6 +240,8 @@
             pltpu.VMEM(pin.shape, BF16),
             pltpu.VMEM(pin.shape, BF16),
             pltpu.VMEM(query.shape, BF16),
+            pltpu.VMEM((query.shape[2] // 128, qpd * held, 128), F32),
+            pltpu.VMEM((held, qpd, query.shape[2]), BF16),
             pltpu.VMEM(bin_.shape, F32),
             pltpu.VMEM(bout.shape, F32),
             pltpu.VMEM((n, rank, held * rank), BF16),
@@ -246,7 +255,7 @@
             pltpu.SemaphoreType.DMA((n,)),
         ],
         compiler_params=pltpu.CompilerParams(
-            collective_id=0, has_side_effects=True, vmem_limit_bytes=48 * 2**20
+            collective_id=0, has_side_effects=True, vmem_limit_bytes=60 * 2**20
         ),
     )(lens, lids, acts, grads, query, pin, pout, bin_, bout)
 

time: 29.4 us -> 23.9 us (0.81)
  local copies, waits for them, and re-layouts: 7.4 us -> 1.19 us
  Pallas kernels: 21 us -> 21.9 us
    unnamed x12 -> x1, local copies, waits for them, and re-layouts: 7.4 us -> 1.19 us
    pallas_call x1, Pallas kernels: 21 us -> 21.9 us  [per_device(): pl.pallas_call(functools.partial(kernel, n, layers), out_shape=jax.ShapeD...]
where the time goes in v2:
time: 23.9 us; the launch traced here: 23.7 us
  Pallas kernels  21.9 us (92%)
  local copies, waits for them, and re-layouts  1.19 us (5%)
  between operations  0.66 us (3%)
    pallas_call x1, Pallas kernels, per_device(): pl.pallas_call(functools.partial(kernel, n, layers), out_shape=jax.ShapeD...  21.9 us
    unnamed x1, local copies, waits for them, and re-layouts  1.19 us

profile of v2, /device:TPU:0, one launch (start us, length us, event | category | flops | bytes accessed | tf_op | source)
XLA Modules:
  0.0 23.7 jit_solution(2700567256543878956)
XLA Ops:
  0.7 21.9 %shard_map.91 = f32[1,128]{1,0:T(1,128)} custom-call(s32[1]{0:T(128)S(6)} %copy.11.lens, s32[2]{0:T(128)} %lids.1, bf16[1,2,256,4096]{3,2,1,0:T(8,128)(2,1)} %acts.1, bf16[1,2,256,4096]{3,2,1,0:T(8,128)(2,1)} %grads.1, bf16[32,2,4096]{2,1,0:T(2,128)(2,1)} %query.1, bf16[2,64,4096]{2,1,0:T(8,128)(2,1)} %pin.1, bf16[2,64,4096]{2,1,0:T(8,128)(2,1)} %pout.1, ...), custom_call_target="tpu_custom_call" | custom-call | tf_op jit(solution)/shard_map/pallas_call | solution.py:232
  22.5 1.2 %copy.12 = f32[1,128]{1,0:T(1,128)} copy(f32[1,128]{1,0:T(1,128)} %shard_map.91) | data formatting | bytes 1024

commit v3 on v2

--- a/solution.py
+++ b/solution.py
@@ -9,6 +9,8 @@
 
 F32 = jnp.float32
 BF16 = jnp.bfloat16
+CHUNK = 256
+WINDOW = 4
 MESH = pl.DeviceIdType.MESH
 NN = (((1,), (0,)), ((), ()))
 NT = (((1,), (1,)), ((), ()))
@@ -27,6 +29,12 @@
     ah, al = split(a)
     bh, bl = split(b)
     return dot(ah, bh, dims) + (dot(ah, bl, dims) + dot(al, bh, dims))
+
+
+def deep3(a, b):
+    ah, al = split(a)
+    bh, bl = split(b)
+    return dot(jnp.concatenate([ah, ah, al], axis=1), jnp.concatenate([bh, bl, bh], axis=0))
 
 
 def kernel(
@@ -54,46 +62,50 @@
                 device_id_type=MESH,
             )
 
-    loads = []
-
-    def load(src, dst):
-        c = pltpu.make_async_copy(src, dst, load_sem.at[len(loads)])
-        c.start()
-        loads.append(c)
-        return c
-
-    lp = []
-    for l in range(2):
-        a = load(pout.at[l], pobuf.at[l])
-        b = load(grads.at[0, l], gbuf.at[l])
-        c = load(pin.at[l], pibuf.at[l])
-        d = load(acts.at[0, l], abuf.at[l])
-        if l == 0:
-            e = (load(bin_, bibuf), load(bout, bobuf))
-        lp.append((a, b, c, d))
-    lq = load(query, xbuf)
+    plan = []
+    for l in range(2):
+        for weights, held, rows, kept in ((pout, pobuf, grads, gbuf), (pin, pibuf, acts, abuf)):
+            plan.append((weights.at[l], held.at[l]))
+            for c in range(0, tokens, CHUNK):
+                plan.append((rows.at[0, l, c:c + CHUNK], kept.at[l, c:c + CHUNK]))
+    plan += [(bin_, bibuf), (bout, bobuf), (query, xbuf)]
+    loads = [
+        pltpu.make_async_copy(src, dst, load_sem.at[i]) for i, (src, dst) in enumerate(plan)
+    ]
+    for copy in loads[:WINDOW]:
+        copy.start()
+    count = [0]
+
+    def landed():
+        i = count[0]
+        loads[i].wait()
+        if i + WINDOW < len(loads):
+            loads[i + WINDOW].start()
+        count[0] = i + 1
 
     length = lens[0]
     live = lax.broadcasted_iota(jnp.int32, (rank, tokens), 1) < length
-    frames_in, frames_out, turned = [], [], []
-    for l in range(2):
-        a, b, c, d = lp[l]
-        a.wait()
-        b.wait()
-        low_out = dot(pobuf[l], gbuf[l], NT)
-        low_out = jnp.where(live, low_out, 0.0)
-        c.wait()
-        d.wait()
-        low_in = dot(abuf[l], pibuf[l], NT)
-        if l == 0:
-            e[0].wait()
-            e[1].wait()
-        v = bibuf[lids[l]]
-        u = bobuf[lids[l]]
-        frames_in.append(v)
-        frames_out.append(u)
-        outer = dot3(low_out, low_in)
-        turned.append(dot3(dot3(u.T, outer), v))
+    lows = []
+    for l in range(2):
+        landed()
+        low_out = []
+        for c in range(0, tokens, CHUNK):
+            landed()
+            low_out.append(dot(pobuf[l], gbuf[l, c:c + CHUNK], NT))
+        landed()
+        low_in = []
+        for c in range(0, tokens, CHUNK):
+            landed()
+            low_in.append(dot(abuf[l, c:c + CHUNK], pibuf[l], NT))
+        low_out = jnp.where(live, jnp.concatenate(low_out, axis=1), 0.0)
+        lows.append((low_out, jnp.concatenate(low_in, axis=0)))
+    outers = [dot3(low_out, low_in) for low_out, low_in in lows]
+    landed()
+    landed()
+    frames_in = [bibuf[lids[l]] for l in range(2)]
+    frames_out = [bobuf[lids[l]] for l in range(2)]
+    lefts = [deep3(frames_out[l].T, outers[l]) for l in range(2)]
+    turned = [dot3(lefts[l], frames_in[l]) for l in range(2)]
     tbuf[me] = jnp.concatenate(turned, axis=1).astype(BF16)
 
     peers = (n * layers) - 1
@@ -122,7 +134,7 @@
     v0 = jnp.concatenate([frames_in[0], zero], axis=1)
     v1 = jnp.concatenate([zero, frames_in[1]], axis=1)
     right = jnp.concatenate([v0, v0, v1, v1], axis=0)
-    lq.wait()
+    landed()
     rows = xbuf[...].reshape(2 * qpd, xbuf.shape[2])
     for j in range(fbuf.shape[0]):
         fbuf[j] = rows[:, j * 128:(j + 1) * 128].astype(F32)
@@ -150,7 +162,7 @@
         yl = jnp.concatenate(
             [y[s * rank:(s + 1) * rank, l * wide:(l + 1) * wide] for s in range(n)], axis=1
         )
-        w = dot3(frames_out[l], yl)
+        w = deep3(frames_out[l], yl)
         for s in range(n):
             wbuf[l, s * rank:(s + 1) * rank, :] = w[:, s * wide:(s + 1) * wide]
         tiles = []
@@ -248,7 +260,7 @@
             pltpu.VMEM((held, n * rank, 2 * rank), F32),
             pltpu.VMEM((n, 1, 128), F32),
             pltpu.VMEM((n, 1, 128), F32),
-            pltpu.SemaphoreType.DMA((11,)),
+            pltpu.SemaphoreType.DMA((4 + 4 * (tokens // CHUNK) + 3,)),
             pltpu.SemaphoreType.DMA((n - 1,)),
             pltpu.SemaphoreType.DMA((n - 1,)),
             pltpu.SemaphoreType.DMA((n,)),

time: 23.9 us -> 23.4 us (0.979)
  Pallas kernels: 21.9 us -> 21.3 us
    pallas_call x1, Pallas kernels: 21.9 us -> 21.3 us  [per_device(): pl.pallas_call(functools.partial(kernel, n, layers), out_shape=jax.ShapeD...]
where the time goes in v3:
time: 23.4 us; the launch traced here: 23.2 us
  Pallas kernels  21.3 us (91%)
  local copies, waits for them, and re-layouts  1.19 us (5%)
  between operations  0.66 us (3%)
    pallas_call x1, Pallas kernels, per_device(): pl.pallas_call(functools.partial(kernel, n, layers), out_shape=jax.ShapeD...  21.3 us
    unnamed x1, local copies, waits for them, and re-layouts  1.19 us

profile of v3, /device:TPU:0, one launch (start us, length us, event | category | flops | bytes accessed | tf_op | source)
XLA Modules:
  0.0 23.2 jit_solution(4648952502254427065)
XLA Ops:
  0.7 21.3 %shard_map.91 = f32[1,128]{1,0:T(1,128)} custom-call(s32[1]{0:T(128)S(6)} %copy.11.lens, s32[2]{0:T(128)} %lids.1, bf16[1,2,256,4096]{3,2,1,0:T(8,128)(2,1)} %acts.1, bf16[1,2,256,4096]{3,2,1,0:T(8,128)(2,1)} %grads.1, bf16[32,2,4096]{2,1,0:T(2,128)(2,1)} %query.1, bf16[2,64,4096]{2,1,0:T(8,128)(2,1)} %pin.1, bf16[2,64,4096]{2,1,0:T(8,128)(2,1)} %pout.1, ...), custom_call_target="tpu_custom_call" | custom-call | tf_op jit(solution)/shard_map/pallas_call | solution.py:244
  22.0 1.2 %copy.12 = f32[1,128]{1,0:T(1,128)} copy(f32[1,128]{1,0:T(1,128)} %shard_map.91) | data formatting | bytes 1024

commit v4 on v3

--- a/solution.py
+++ b/solution.py
@@ -38,9 +38,9 @@
 
 
 def kernel(
-    n, layers, lens, lids, acts, grads, query, pin, pout, bin_, bout, out,
+    n, layers, lens_hbm, lids_hbm, acts, grads, query, pin, pout, bin_, bout, out,
     abuf, gbuf, pibuf, pobuf, xbuf, fbuf, qbuf, bibuf, bobuf, tbuf, wbuf, sbuf, rbuf,
-    load_sem, send_sem, recv_sem, send2_sem, recv2_sem,
+    lens, lids, id_sem, load_sem, send_sem, recv_sem, send2_sem, recv2_sem,
 ):
     part = lax.axis_index("parts")
     me = lax.axis_index("dp")
@@ -51,6 +51,22 @@
     qpd = query.shape[0]
     tokens = abuf.shape[1]
 
+    plan = []
+    for l in range(2):
+        for weights, held, rows, kept in ((pout, pobuf, grads, gbuf), (pin, pibuf, acts, abuf)):
+            plan.append((weights.at[l], held.at[l]))
+            for c in range(0, tokens, CHUNK):
+                plan.append((rows.at[0, l, c:c + CHUNK], kept.at[l, c:c + CHUNK]))
+    plan += [(bin_, bibuf), (bout, bobuf), (query, xbuf)]
+    loads = [
+        pltpu.make_async_copy(src, dst, load_sem.at[i]) for i, (src, dst) in enumerate(plan)
+    ]
+    ids = [
+        pltpu.make_async_copy(lens_hbm, lens, id_sem.at[0]),
+        pltpu.make_async_copy(lids_hbm, lids, id_sem.at[1]),
+    ]
+    for copy in ids + loads[:WINDOW]:
+        copy.start()
     barrier = pltpu.get_barrier_semaphore()
     for off in range(n):
         for lay in range(layers):
@@ -62,18 +78,6 @@
                 device_id_type=MESH,
             )
 
-    plan = []
-    for l in range(2):
-        for weights, held, rows, kept in ((pout, pobuf, grads, gbuf), (pin, pibuf, acts, abuf)):
-            plan.append((weights.at[l], held.at[l]))
-            for c in range(0, tokens, CHUNK):
-                plan.append((rows.at[0, l, c:c + CHUNK], kept.at[l, c:c + CHUNK]))
-    plan += [(bin_, bibuf), (bout, bobuf), (query, xbuf)]
-    loads = [
-        pltpu.make_async_copy(src, dst, load_sem.at[i]) for i, (src, dst) in enumerate(plan)
-    ]
-    for copy in loads[:WINDOW]:
-        copy.start()
     count = [0]
 
     def landed():
@@ -83,6 +87,8 @@
             loads[i + WINDOW].start()
         count[0] = i + 1
 
+    for copy in ids:
+        copy.wait()
     length = lens[0]
     live = lax.broadcasted_iota(jnp.int32, (rank, tokens), 1) < length
     lows = []
@@ -240,11 +246,10 @@
     rank = pin.shape[1]
     qpd = query.shape[0]
     hbm = pl.BlockSpec(memory_space=pl.ANY)
-    smem = pl.BlockSpec(memory_space=pltpu.SMEM)
     return pl.pallas_call(
         functools.partial(kernel, n, layers),
         out_shape=jax.ShapeDtypeStruct((1, n * qpd // layers), F32),
-        in_specs=[smem, smem] + [hbm] * 7,
+        in_specs=[hbm] * 9,
         out_specs=pl.BlockSpec(memory_space=pltpu.VMEM),
         scratch_shapes=[
             pltpu.VMEM((held, tokens, width), BF16),
@@ -260,6 +265,9 @@
             pltpu.VMEM((held, n * rank, 2 * rank), F32),
             pltpu.VMEM((n, 1, 128), F32),
             pltpu.VMEM((n, 1, 128), F32),
+            pltpu.SMEM(lens.shape, jnp.int32),
+            pltpu.SMEM(lids.shape, jnp.int32),
+            pltpu.SemaphoreType.DMA((2,)),
             pltpu.SemaphoreType.DMA((4 + 4 * (tokens // CHUNK) + 3,)),
             pltpu.SemaphoreType.DMA((n - 1,)),
             pltpu.SemaphoreType.DMA((n - 1,)),

time: 23.4 us -> 22.6 us (0.966)
  Pallas kernels: 21.3 us -> 20.5 us
    pallas_call x1, Pallas kernels: 21.3 us -> 20.5 us  [per_device(): pl.pallas_call(functools.partial(kernel, n, layers), out_shape=jax.ShapeD...]
where the time goes in v4:
time: 22.6 us; the launch traced here: 22.4 us
  Pallas kernels  20.5 us (91%)
  local copies, waits for them, and re-layouts  1.19 us (5%)
  between operations  0.66 us (3%)
    pallas_call x1, Pallas kernels, per_device(): pl.pallas_call(functools.partial(kernel, n, layers), out_shape=jax.ShapeD...  20.5 us
    unnamed x1, local copies, waits for them, and re-layouts  1.19 us

profile of v4, /device:TPU:0, one launch (start us, length us, event | category | flops | bytes accessed | tf_op | source)
XLA Modules:
  0.0 22.4 jit_solution(14430261588931452846)
XLA Ops:
  0.7 20.5 %shard_map.91 = f32[1,128]{1,0:T(1,128)} custom-call(s32[1]{0:T(128)S(6)} %copy.11.lens_hbm, s32[2]{0:T(128)} %lids_hbm.1, bf16[1,2,256,4096]{3,2,1,0:T(8,128)(2,1)} %acts.1, bf16[1,2,256,4096]{3,2,1,0:T(8,128)(2,1)} %grads.1, bf16[32,2,4096]{2,1,0:T(2,128)(2,1)} %query.1, bf16[2,64,4096]{2,1,0:T(8,128)(2,1)} %pin.1, bf16[2,64,4096]{2,1,0:T(8,128)(2,1)} %pout.1, ...), custom_call_target="tpu_custom_call" | custom-call | tf_op jit(solution)/shard_map/pallas_call | solution.py:249
  21.2 1.2 %copy.12 = f32[1,128]{1,0:T(1,128)} copy(f32[1,128]{1,0:T(1,128)} %shard_map.91) | data formatting | bytes 1024

commit v5 on v4

--- a/solution.py
+++ b/solution.py
@@ -139,7 +139,8 @@
     zero = jnp.zeros((rank, rank), F32)
     v0 = jnp.concatenate([frames_in[0], zero], axis=1)
     v1 = jnp.concatenate([zero, frames_in[1]], axis=1)
-    right = jnp.concatenate([v0, v0, v1, v1], axis=0)
+    right_hi, right_lo = split(jnp.concatenate([v0, v0, v1, v1], axis=0))
+    right_twice = jnp.concatenate([right_hi, right_hi], axis=1)
     landed()
     rows = xbuf[...].reshape(2 * qpd, xbuf.shape[2])
     for j in range(fbuf.shape[0]):
@@ -160,7 +161,8 @@
     sum1 = jnp.sum(jnp.where(first, 0.0, energy))
     damping = jnp.where(first, sum0, sum1) * (0.1 / (rank * rank)) + 1e-6
     scaled = t * (1.0 / (energy + damping))[None]
-    y = dot3(scaled.reshape(n * rank, 2 * rank), right, NT)
+    sh, sl = split(scaled.reshape(n * rank, 2 * rank))
+    y = dot(jnp.concatenate([sh, sl], axis=1), right_twice, NT) + dot(sh, right_lo, NT)
     wide = 2 * rank
     lanes = lax.broadcasted_iota(jnp.int32, (n, wide), 1) < rank
     total = None

time: 22.6 us -> 22.4 us (level)
  no operation moved by 1% of the time
where the time goes in v5:
time: 22.4 us; the launch traced here: 22.2 us
  Pallas kernels  20.3 us (91%)
  local copies, waits for them, and re-layouts  1.19 us (5%)
  between operations  0.66 us (3%)
    pallas_call x1, Pallas kernels, per_device(): pl.pallas_call(functools.partial(kernel, n, layers), out_shape=jax.ShapeD...  20.3 us
    unnamed x1, local copies, waits for them, and re-layouts  1.19 us

profile of v5, /device:TPU:0, one launch (start us, length us, event | category | flops | bytes accessed | tf_op | source)
XLA Modules:
  0.0 22.2 jit_solution(15179594815163137344)
XLA Ops:
  0.7 20.3 %shard_map.91 = f32[1,128]{1,0:T(1,128)} custom-call(s32[1]{0:T(128)S(6)} %copy.11.lens_hbm, s32[2]{0:T(128)} %lids_hbm.1, bf16[1,2,256,4096]{3,2,1,0:T(8,128)(2,1)} %acts.1, bf16[1,2,256,4096]{3,2,1,0:T(8,128)(2,1)} %grads.1, bf16[32,2,4096]{2,1,0:T(2,128)(2,1)} %query.1, bf16[2,64,4096]{2,1,0:T(8,128)(2,1)} %pin.1, bf16[2,64,4096]{2,1,0:T(8,128)(2,1)} %pout.1, ...), custom_call_target="tpu_custom_call" | custom-call | tf_op jit(solution)/shard_map/pallas_call | solution.py:251
  21.0 1.2 %copy.12 = f32[1,128]{1,0:T(1,128)} copy(f32[1,128]{1,0:T(1,128)} %shard_map.91) | data formatting | bytes 1024
